TPU v7x, 32 devices: a whole 2x2x4 slice. The times are simulated.
32 devices in a mesh: ctx: 8 (over z, y), head: 4 (over x, core).
Axes of the slice: x: 2, y: 2, z: 4, core: 2. Of those that a mesh axis runs over, the one named last changes fastest.
Arguments:
- queries: bfloat16 [1024, 64, 576], P('ctx', 'head'), may hold values from -100 to 100
- latent_cache: bfloat16 [16, 36864], P('ctx'), may hold values from -6 to 6
- selected: int32 [16, 8], P('ctx'), may hold values from -1 to 15, as said below
- value_weight: bfloat16 [64, 512, 128], P('head'), may hold values from -0.25 to 0.25
Outputs:
- attended: bfloat16 [1024, 8192], P(('ctx', 'head'))
Inputs may be any that keep to these rules, and one draw needn't show every extreme that they name: `selected`: row b lists distinct key blocks: its first entry is b itself, the others lie below b; where b + 1 < 8 the row holds all of 0 to b and its remaining slots are -1.
All inputs are finite; a program needn't handle non-finite values.
Results may differ from a plain program's by a relative error of at most 0.011.
Values may be sent and summed in bfloat16 or wider, within the bound.
A program may use at most 64 MiB of HBM per device.

v0:
```python
import functools
import math

import jax
import jax.numpy as jnp
from jax import lax
from jax.experimental import pallas as pl
from jax.experimental.pallas import tpu as pltpu
from jax.sharding import PartitionSpec as P

DC = 512
DR = 64
DV = 128
KBLK = 64
SEL = 8
GROUPS = 4
MESH = pl.DeviceIdType.MESH
FAR = 1 << 30
VMEM_LIMIT = 52 * 1024 * 1024


def kernel(
    n_ctx, n_head, heads,
    sel_hbm, own_ref, q_hbm, w_hbm, out_ref,
    sel_ref, keys, kbuf, q_ref, q_blocks, w_ref, stage,
    load_sem, s_pair, s_side, s1, r1, s2, r2, s3, r3, s4, r4, s_out, r_out, l_out,
):
    c = lax.axis_index("ctx")
    h = lax.axis_index("head")
    plane, side = c // 2, c % 2
    c_pair = 2 * plane + (1 - side)
    x, core = h // 2, h % 2
    h_core = 2 * x + (1 - core)
    h_x = 2 * (1 - x) + core
    h_diag = 2 * (1 - x) + (1 - core)
    own_rows = own_ref.shape[0]
    blocks = own_rows // KBLK
    part = own_rows // n_head

    load_q = pltpu.make_async_copy(q_hbm, q_ref, load_sem.at[0])
    load_w = pltpu.make_async_copy(w_hbm, w_ref, load_sem.at[1])
    load_sel = pltpu.make_async_copy(sel_hbm, sel_ref, load_sem.at[2])
    load_q.start()
    load_sel.start()
    load_w.start()

    barrier = pltpu.get_barrier_semaphore()
    for peer in (h_core, h_x, h_diag):
        pl.semaphore_signal(barrier, inc=1, device_id=(c, peer), device_id_type=MESH)

    for peer in (h, h_x):
        pl.semaphore_signal(barrier, inc=1, device_id=(c_pair, peer), device_id_type=MESH)

    @pl.loop(0, plane)
    def _(lower):
        pl.semaphore_signal(barrier, inc=1, device_id=(2 * lower + side, h), device_id_type=MESH)

    above = n_ctx // 2 - 1 - plane
    pl.semaphore_wait(barrier, 5 + above)

    def piece(source, quarter):
        row = quarter * part
        start = pl.multiple_of(row % KBLK, part)
        return keys.at[source * blocks + row // KBLK, pl.ds(start, part), :]

    def first_copy(source, target):
        return pltpu.make_async_remote_copy(
            src_ref=own_ref.at[pl.ds(pl.multiple_of(h * part, part), part), :],
            dst_ref=piece(source, h),
            send_sem=s1.at[target], recv_sem=r1.at[source],
            device_id=(target, h), device_id_type=MESH,
        )

    def pair_copy(source, quarter, send, recv):
        return pltpu.make_async_remote_copy(
            src_ref=own_ref.at[pl.ds(pl.multiple_of(quarter * part, part), part), :],
            dst_ref=piece(source, quarter),
            send_sem=s_pair.at[send], recv_sem=recv.at[source],
            device_id=(c_pair, h), device_id_type=MESH,
        )

    def side_copy(source, peer, send, recv):
        return pltpu.make_async_remote_copy(
            src_ref=piece(source, h), dst_ref=piece(source, h),
            send_sem=s_side.at[send, source], recv_sem=recv.at[source],
            device_id=(c_pair, peer), device_id_type=MESH,
        )

    def relay(source, quarter, peer, send, recv):
        return pltpu.make_async_remote_copy(
            src_ref=piece(source, quarter), dst_ref=piece(source, quarter),
            send_sem=send.at[source], recv_sem=recv.at[source],
            device_id=(c, peer), device_id_type=MESH,
        )

    @pl.when(side == 0)
    def _():
        pair_copy(c, h, 0, r1).start()
        pair_copy(c, h_x, 1, r2).start()

    @pl.loop(0, above)
    def _(step):
        first_copy(c, n_ctx - 2 + side - 2 * step).start()

    for block in range(blocks):
        keys[c * blocks + block] = own_ref[block * KBLK:(block + 1) * KBLK, :]

    load_q.wait()
    per_group = heads // GROUPS
    columns = per_group * KBLK
    for pair in range(heads // 2):
        group, slot = divmod(pair, heads // (2 * GROUPS))
        lanes = slice(slot * 2 * KBLK, (slot + 1) * 2 * KBLK)
        first, second = q_ref[2 * pair], q_ref[2 * pair + 1]
        q_blocks[0, group, :, lanes] = jnp.concatenate([first[:, :KBLK], second[:, :KBLK]], axis=1)
        q_blocks[1, group, :, lanes] = jnp.concatenate([first[:, KBLK:], second[:, KBLK:]], axis=1)

    def pass_first(source):
        first_copy(source, c).wait_recv()
        relay(source, h, h_core, s3, r3).start()

    def pass_second(source):
        relay(source, h_x, h_x, s2, r2).wait_recv()
        relay(source, h_x, h_core, s4, r4).start()

    def complete(source):
        relay(source, h_core, h_core, s3, r3).wait_recv()
        relay(source, h_diag, h_core, s4, r4).wait_recv()

    def same(step):
        return 2 * (plane - 1 - step) + side

    def other(step):
        return 2 * (plane - step) + (1 - side)

    def has_same(step):
        return (step >= 0) & (step < plane)

    def has_other(step):
        return (step >= 1 - side) & (step <= plane)

    @pl.loop(0, plane + 3)
    def _(step):
        @pl.when(has_same(step))
        def _():
            source = same(step)
            first_copy(source, c).wait_recv()
            side_copy(source, h, 0, r1).start()
            side_copy(source, h_x, 1, r2).start()
            relay(source, h, h_x, s2, r2).start()
            relay(source, h, h_core, s3, r3).start()

        @pl.when(has_other(step - 1))
        def _():
            pass_first(other(step - 1))
            pass_second(other(step - 1))

        @pl.when(has_same(step - 2))
        def _():
            pass_second(same(step - 2))

        @pl.when(has_other(step - 2))
        def _():
            complete(other(step - 2))

        @pl.when(has_same(step - 3))
        def _():
            complete(same(step - 3))

    load_w.wait()
    load_sel.wait()

    factor = (DV + DR) ** (-0.5) * math.log2(math.e)
    key_row = lax.broadcasted_iota(jnp.int32, (SEL * KBLK, 1), 0)
    width = per_group * DV
    token = lax.broadcasted_iota(jnp.int32, (1, columns), 1) % KBLK

    def out_copy(group, target, relation):
        return pltpu.make_async_remote_copy(
            src_ref=stage.at[target, :, pl.ds(group * width, width)],
            dst_ref=out_ref.at[:, pl.ds(pl.multiple_of(h * (heads * DV) + group * width, width), width)],
            send_sem=s_out.at[relation, group], recv_sem=r_out.at[relation, group],
            device_id=(c, target), device_id_type=MESH,
        )

    def out_local(group):
        return pltpu.make_async_copy(
            stage.at[h, :, pl.ds(group * width, width)],
            out_ref.at[:, pl.ds(pl.multiple_of(h * (heads * DV) + group * width, width), width)],
            l_out.at[group],
        )

    half = KBLK // 2

    def slots_of(position):
        chosen = [sel_ref[position, slot] for slot in range(SEL)]
        return chosen, [jnp.maximum(one, 0) for one in chosen]

    def weigh(turn, position, group):
        chosen, _ = slots_of(position)
        key_block = jnp.full((SEL * KBLK, 1), chosen[0], jnp.int32)
        for slot in range(1, SEL):
            key_block = jnp.where(key_row // KBLK == slot, chosen[slot], key_block)
        key_place = jnp.where(key_block < 0, FAR, key_block * KBLK + key_row % KBLK)
        query_place = token + (c * blocks + position) * KBLK
        scores = jnp.dot(kbuf[turn], q_blocks[position, group], preferred_element_type=jnp.float32)
        scores = jnp.where(key_place <= query_place, scores, -1e30)
        largest = jnp.max(scores, axis=0, keepdims=True)
        powered = jnp.exp2((scores - largest) * factor)
        total = jnp.sum(powered, axis=0, keepdims=True)
        return (powered * (1.0 / total)).astype(jnp.bfloat16).T

    def finish(turn, position, group, weights):
        latent = jnp.dot(weights, kbuf[turn, :, :DC], preferred_element_type=jnp.float32).astype(jnp.bfloat16)
        for inner in range(per_group):
            head = group * per_group + inner
            value = jnp.dot(
                latent[inner * KBLK:(inner + 1) * KBLK], w_ref[head], preferred_element_type=jnp.float32
            ).astype(jnp.bfloat16)
            stage[2 * position, :, head * DV:(head + 1) * DV] = value[:half]
            stage[2 * position + 1, :, head * DV:(head + 1) * DV] = value[half:]

    def send(turn, group):
        if turn == 0:
            out_copy(group, h_x, 0).start()
            out_copy(group, h_diag, 1).start()
        else:
            out_copy(group, h_core, 2).start()
            out_local(group).start()

    order = [(turn, (1 - x) if turn == 0 else x, group) for turn in range(2) for group in range(GROUPS)]
    for turn in range(2):
        _, entry = slots_of((1 - x) if turn == 0 else x)
        for slot in range(SEL):
            kbuf[turn, slot * KBLK:(slot + 1) * KBLK, :] = keys[entry[slot]]
    weights = weigh(*order[0])
    for number, (turn, position, group) in enumerate(order):
        after = None
        if number + 1 < len(order):
            after = weigh(*order[number + 1])
        finish(turn, position, group, weights)
        send(turn, group)
        weights = after

    for group in range(GROUPS):
        out_local(group).wait()
        for relation, peer in enumerate((h_x, h_diag, h_core)):
            out_copy(group, peer, relation).wait()

    @pl.when(side == 0)
    def _():
        pair_copy(c, h, 0, r1).wait_send()
        pair_copy(c, h_x, 1, r2).wait_send()

    @pl.loop(0, above)
    def _(step):
        first_copy(c, n_ctx - 2 + side - 2 * step).wait_send()

    @pl.loop(0, c)
    def _(source):
        relay(source, h, h_core, s3, r3).wait_send()
        relay(source, h_x, h_core, s4, r4).wait_send()

    @pl.loop(0, plane)
    def _(lower):
        source = 2 * lower + side
        relay(source, h, h_x, s2, r2).wait_send()
        side_copy(source, h, 0, r1).wait_send()
        side_copy(source, h_x, 1, r2).wait_send()


def per_device(queries, latent_cache, selected, value_weight):
    n_ctx, n_head = lax.axis_size("ctx"), lax.axis_size("head")
    width = DC + DR
    tokens, heads = queries.shape[:2]
    own = latent_cache.reshape(tokens, width)
    by_head = queries.transpose(1, 2, 0)
    part = tokens // n_head
    dma = pltpu.SemaphoreType.DMA
    return pl.pallas_call(
        functools.partial(kernel, n_ctx, n_head, heads),
        out_shape=jax.ShapeDtypeStruct((part, n_head * heads * DV), jnp.bfloat16),
        in_specs=[
            pl.BlockSpec(memory_space=pltpu.HBM),
            pl.BlockSpec(memory_space=pltpu.VMEM),
            pl.BlockSpec(memory_space=pl.ANY),
            pl.BlockSpec(memory_space=pl.ANY),
        ],
        out_specs=pl.BlockSpec(memory_space=pl.ANY),
        scratch_shapes=[
            pltpu.SMEM(selected.shape, jnp.int32),
            pltpu.VMEM((n_ctx * tokens // KBLK, KBLK, width), jnp.bfloat16),
            pltpu.VMEM((2, SEL * KBLK, width), jnp.bfloat16),
            pltpu.VMEM((heads, width, tokens), jnp.bfloat16),
            pltpu.VMEM((tokens // KBLK, GROUPS, width, heads // GROUPS * KBLK), jnp.bfloat16),
            pltpu.VMEM((heads, DC, DV), jnp.bfloat16),
            pltpu.VMEM((n_head, part, heads * DV), jnp.bfloat16),
            dma((3,)), dma((2,)), dma((2, n_ctx)),
            dma((n_ctx,)), dma((n_ctx,)),
            dma((n_ctx,)), dma((n_ctx,)),
            dma((n_ctx,)), dma((n_ctx,)),
            dma((n_ctx,)), dma((n_ctx,)),
            dma((3, GROUPS)), dma((3, GROUPS)), dma((GROUPS,)),
        ],
        compiler_params=pltpu.CompilerParams(
            collective_id=0, has_side_effects=True, vmem_limit_bytes=VMEM_LIMIT
        ),
    )(selected, own, by_head, value_weight)


def solution(mesh):
    in_specs = (P("ctx", "head", None), P("ctx", None), P("ctx", None), P("head", None, None))
    out_specs = P(("ctx", "head"), None)
    return jax.shard_map(
        per_device, mesh=mesh, in_specs=in_specs, out_specs=out_specs, check_vma=False
    )
```

profile of v0, /device:TPU:16, one launch (start us, length us, event | category | flops | bytes accessed | tf_op | source)
XLA Modules:
  0.0 25.3 jit_solution(11323819851485046401)
XLA Ops:
  0.0 1.1 %reshape.3.own_ref = bf16[128,576]{1,0:T(8,128)(2,1)S(1)} reshape(bf16[2,36864]{1,0:T(2,128)(2,1)} %param.5) | data formatting | bytes 294912 | tf_op jit(solution)/shard_map/reshape | solution.py:276
  1.1 0.0 copy-start
  1.1 0.7 %copy-done = s32[2,8]{1,0:T(2,128)S(1)} copy-done((s32[2,8]{1,0:T(2,128)S(1)}, s32[2,8]{1,0:T(2,128)}, u32[]{:S(2)}) %copy-start) | copy-done | bytes 88
  1.8 22.7 %shard_map.46 = bf16[32,8192]{1,0:T(8,128)(2,1)S(1)} custom-call(s32[2,8]{1,0:T(2,128)S(1)} %copy-done, bf16[128,576]{1,0:T(8,128)(2,1)S(1)} %reshape.3.own_ref, bf16[16,576,128]{2,1,0:T(8,128)(2,1)} %bitcast.1, bf16[16,512,128]{2,1,0:T(8,128)(2,1)} %w_hbm.1), custom_call_target="tpu_custom_call" | custom-call | tf_op jit(solution)/shard_map/pallas_call | solution.py:280
  24.5 0.8 %copy.6 = bf16[32,8192]{1,0:T(8,128)(2,1)} copy(bf16[32,8192]{1,0:T(8,128)(2,1)S(1)} %shard_map.46) | data formatting | bytes 1048576
Async XLA Ops:
  1.1 0.7 %copy-start = (s32[2,8]{1,0:T(2,128)S(1)}, s32[2,8]{1,0:T(2,128)}, u32[]{:S(2)}) copy-start(s32[2,8]{1,0:T(2,128)} %sel_hbm.1) | copy-start | bytes 196
where the time goes:
time: 25.5 us; the launch traced here: 25.3 us
  Pallas kernels  22.7 us (89%)
  local copies, waits for them, and re-layouts  2.58 us (10%)
    pallas_call x1, Pallas kernels, per_device(): pl.pallas_call(functools.partial(kernel, n_ctx, n_head, heads), out_shape...  22.7 us
    unnamed x3, local copies, waits for them, and re-layouts  1.47 us
    reshape x1, local copies, waits for them, and re-layouts, per_device(): own = latent_cache.reshape(tokens, width)  1.1 us

commit v1 on v0

--- a/solution.py
+++ b/solution.py
@@ -14,6 +14,7 @@
 KBLK = 64
 SEL = 8
 GROUPS = 4
+STORES = 4
 MESH = pl.DeviceIdType.MESH
 FAR = 1 << 30
 VMEM_LIMIT = 52 * 1024 * 1024
@@ -229,13 +230,18 @@
             out_local(group).start()
 
     order = [(turn, (1 - x) if turn == 0 else x, group) for turn in range(2) for group in range(GROUPS)]
-    for turn in range(2):
-        _, entry = slots_of((1 - x) if turn == 0 else x)
+
+    def assemble(turn, position):
+        _, entry = slots_of(position)
         for slot in range(SEL):
             kbuf[turn, slot * KBLK:(slot + 1) * KBLK, :] = keys[entry[slot]]
+
+    assemble(0, 1 - x)
     weights = weigh(*order[0])
     for number, (turn, position, group) in enumerate(order):
         after = None
+        if number == 0:
+            assemble(1, x)
         if number + 1 < len(order):
             after = weigh(*order[number + 1])
         finish(turn, position, group, weights)
@@ -267,6 +273,20 @@
         relay(source, h, h_x, s2, r2).wait_send()
         side_copy(source, h, 0, r1).wait_send()
         side_copy(source, h_x, 1, r2).wait_send()
+
+
+def store(landed, out_ref, sems):
+    span = landed.shape[1] // STORES
+    copies = [
+        pltpu.make_async_copy(
+            landed.at[:, pl.ds(index * span, span)], out_ref.at[:, pl.ds(index * span, span)], sems.at[index]
+        )
+        for index in range(STORES)
+    ]
+    for copy in copies:
+        copy.start()
+    for copy in copies:
+        copy.wait()
 
 
 def per_device(queries, latent_cache, selected, value_weight):
@@ -277,7 +297,8 @@
     by_head = queries.transpose(1, 2, 0)
     part = tokens // n_head
     dma = pltpu.SemaphoreType.DMA
-    return pl.pallas_call(
+    chosen = jnp.maximum(selected, -1)
+    landed = pl.pallas_call(
         functools.partial(kernel, n_ctx, n_head, heads),
         out_shape=jax.ShapeDtypeStruct((part, n_head * heads * DV), jnp.bfloat16),
         in_specs=[
@@ -305,7 +326,14 @@
         compiler_params=pltpu.CompilerParams(
             collective_id=0, has_side_effects=True, vmem_limit_bytes=VMEM_LIMIT
         ),
-    )(selected, own, by_head, value_weight)
+    )(chosen, own, by_head, value_weight)
+    return pl.pallas_call(
+        store,
+        out_shape=jax.ShapeDtypeStruct(landed.shape, landed.dtype),
+        in_specs=[pl.BlockSpec(memory_space=pl.ANY)],
+        out_specs=pl.BlockSpec(memory_space=pl.ANY),
+        scratch_shapes=[dma((STORES,))],
+    )(landed)
 
 
 def solution(mesh):

time: 25.5 us -> 42.5 us (1.67)
  the two profiles are of different devices: /device:TPU:16 before, /device:TPU:17 now
where the time goes in v1:
time: 42.5 us; the launch traced here: 42 us
  Pallas kernels  39.4 us (93%)
  local copies, waits for them, and re-layouts  1.88 us (4%)
  other arithmetic  0.68 us (2%)
    pallas_call x1, Pallas kernels, per_device(): pl.pallas_call(functools.partial(kernel, n_ctx, n_head, heads), out_shape...  22.4 us
    pallas_call x1, Pallas kernels, per_device(): pl.pallas_call(store, out_shape=jax.ShapeDtypeStruct(landed.shape, landed...  17 us
    reshape x1, local copies, waits for them, and re-layouts, per_device(): own = latent_cache.reshape(tokens, width)  1.1 us

profile of v1, /device:TPU:17, one launch (start us, length us, event | category | flops | bytes accessed | tf_op | source)
XLA Modules:
  0.0 42.0 jit_solution(11645692501807709781)
XLA Ops:
  0.0 0.7 %broadcast_maximum_fusion.sel_hbm = s32[2,8]{1,0:T(2,128)S(1)} fusion(s32[2,8]{1,0:T(2,128)} %param.6), kind=kLoop, calls=%fused_computation | loop fusion | flops 16 | bytes 128 | tf_op jit(solution)/shard_map/max | solution.py:300
  0.7 1.1 %reshape.3.own_ref = bf16[128,576]{1,0:T(8,128)(2,1)S(1)} reshape(bf16[2,36864]{1,0:T(2,128)(2,1)} %param.5) | data formatting | bytes 294912 | tf_op jit(solution)/shard_map/reshape | solution.py:296
  1.8 22.4 %shard_map.46.landed = bf16[32,8192]{1,0:T(8,128)(2,1)S(1)} custom-call(s32[2,8]{1,0:T(2,128)S(1)} %broadcast_maximum_fusion.sel_hbm, bf16[128,576]{1,0:T(8,128)(2,1)S(1)} %reshape.3.own_ref, bf16[16,576,128]{2,1,0:T(8,128)(2,1)} %bitcast.1, bf16[16,512,128]{2,1,0:T(8,128)(2,1)} %w_hbm.1), custom_call_target="tpu_custom_call" | custom-call | tf_op jit(solution)/shard_map/pallas_call | solution.py:301
  24.2 0.0 copy-start
  24.2 0.8 %copy-done = bf16[32,8192]{1,0:T(8,128)(2,1)} copy-done((bf16[32,8192]{1,0:T(8,128)(2,1)}, bf16[32,8192]{1,0:T(8,128)(2,1)S(1)}, u32[]{:S(2)}) %copy-start) | copy-done | bytes 524312
  25.0 17.0 %shard_map.47 = bf16[32,8192]{1,0:T(8,128)(2,1)} custom-call(bf16[32,8192]{1,0:T(8,128)(2,1)} %copy-done), custom_call_target="tpu_custom_call" | custom-call | tf_op jit(solution)/shard_map/pallas_call | solution.py:330
Async XLA Ops:
  24.2 0.8 %copy-start = (bf16[32,8192]{1,0:T(8,128)(2,1)}, bf16[32,8192]{1,0:T(8,128)(2,1)S(1)}, u32[]{:S(2)}) copy-start(bf16[32,8192]{1,0:T(8,128)(2,1)S(1)} %shard_map.46.landed) | copy-start | bytes 1572868
